TPU v7x, 32 devices: a whole 2x2x4 slice. The times are simulated.
32 devices in a mesh: tile: 8 (over y, x, core), ens: 4 (over z).
Axes of the slice: x: 2, y: 2, z: 4, core: 2. Of those that a mesh axis runs over, the one named last changes fastest.
Arguments:
- residual: float32 [8, 64, 128], P('ens', 'tile'), may hold values from -6 to 6
- kernel: float32 [64, 8, 128], P('tile'), may hold values from 0.2 to 2
- dest_tile: int32 [64, 1], P('tile'), may hold values from 0 to 7; in each aligned block of 8 rows (0 to 7, 8 to 15, ...) at most 2 rows name the same one
- cell_ids: int32 [64, 128], P('tile'), may hold values from 0 to 8191
- wind_x: float32 [8, 8, 128, 512], P('ens', None, 'tile'), may hold values from -0.5 to 0.5
- wind_y: float32 [8, 8, 128, 512], P('ens', None, 'tile'), may hold values from -0.2 to 0.2
- mixing: float32 [8, 8, 128, 512], P('ens', None, 'tile'), may hold values from 0.01 to 0.15
- sources: int32 [16], replicated, may hold values from 0 to 65535
- gram_matrix: float32 [16, 16], replicated, as said below
Outputs:
- gradient: float32 [128, 512], P('tile', 'ens')
- coefficients: float32 [16], replicated
- adjoint: float32 [8, 8, 128, 512], P('ens', None, 'tile')
Inputs may be any that keep to these rules, and one draw needn't show every extreme that they name: `dest_tile`: among the blocks held by one tile device, at most 2 share a footprint tile, and some footprint tile gets exactly 2 of them on every device. `gram_matrix`: symmetric and strictly diagonally dominant with a positive diagonal.
All inputs are finite; a program needn't handle non-finite values.
Results may differ from a plain program's by a relative error of at most 0.00013.
Values sent between devices are 32-bit elements; how exact they have to be, the bound alone decides.
A program may use at most 64 MiB of HBM per device.

v0:
```python
import jax
import jax.numpy as jnp
from jax import lax
from jax.sharding import PartitionSpec as P

NY = 512
CAP = 2
STEPS = 6


def with_halo(shard, sides, width):
    for axis, dim in sides:
        size, length = (lax.axis_size(axis), shard.shape[dim])
        up = [(i, (i + 1) % size) for i in range(size - 1)]
        down = [(j, i) for i, j in up]
        last = lax.slice_in_dim(shard, length - width, length, axis=dim)
        initial = lax.slice_in_dim(shard, 0, width, axis=dim)
        before = lax.ppermute(last, axis, up)
        after = lax.ppermute(initial, axis, down)
        shard = jnp.concatenate([before, shard, after], axis=dim)
    return shard


def advance(adjoint, speed_x, speed_y, diffusion):
    center = adjoint[:, :, 1:-1]
    next_row = adjoint[:, :, 2:]
    prev_row = adjoint[:, :, :-2]
    along_x = jnp.maximum(speed_x, 0.0) * (next_row - center) + jnp.maximum(-speed_x, 0.0) * (
        prev_row - center
    )
    zero_col = jnp.zeros_like(center[..., :1])
    right_col = jnp.concatenate([center[..., 1:], zero_col], axis=-1)
    left_col = jnp.concatenate([zero_col, center[..., :-1]], axis=-1)
    along_y = jnp.maximum(speed_y, 0.0) * (right_col - center) + jnp.maximum(-speed_y, 0.0) * (
        left_col - center
    )
    level_flux = diffusion[:, :-1] * (center[:, 1:] - center[:, :-1])
    zero_lev = jnp.zeros_like(center[:, :1])
    vertical = jnp.concatenate([level_flux, zero_lev], axis=1) - jnp.concatenate(
        [zero_lev, level_flux], axis=1
    )
    return center + along_x + along_y + vertical


def place_cells(values, cell_index, members, levels, rows_x, columns):
    flat_values = jnp.transpose(values, (1, 2, 0, 3)).reshape(members * levels, -1)
    flat_cells = cell_index.reshape(-1)
    row_table = (
        flat_cells[:, None] // columns == jnp.arange(rows_x, dtype=jnp.int32)[None, :]
    ).astype(jnp.float32)
    col_table = (
        flat_cells[:, None] % columns == jnp.arange(columns, dtype=jnp.int32)[None, :]
    ).astype(jnp.float32)
    weighted = flat_values[:, :, None] * row_table[None, :, :]
    placed = jnp.einsum(
        "arx,ry->axy",
        weighted,
        col_table,
        precision=lax.Precision.HIGHEST,
        preferred_element_type=jnp.float32,
    )
    return placed.reshape(members, levels, rows_x * columns)


def per_device(residual, kernel, dest_tile, cell_ids, wind_x, wind_y, mixing, sources, gram_matrix):
    tiles = lax.axis_size("tile")
    members, levels, rows_x, columns = wind_x.shape
    blocks, row_count = cell_ids.shape
    destination = dest_tile[:, 0]
    one_hot = (destination[:, None] == jnp.arange(tiles, dtype=jnp.int32)[None, :]).astype(
        jnp.int32
    )
    earlier = jnp.cumsum(one_hot, axis=0) - one_hot
    slot_rank = jnp.sum(earlier * one_hot, axis=1)
    position = destination * CAP + slot_rank
    slots = tiles * CAP
    select_int = (jnp.arange(slots, dtype=jnp.int32)[:, None] == position[None, :]).astype(
        jnp.int32
    )
    select = select_int.astype(jnp.float32)
    id_buffer = jnp.sum(select_int[:, :, None] * cell_ids[None, :, :], axis=1).reshape(
        tiles, CAP, row_count
    )
    by_block = jnp.transpose(residual, (1, 0, 2))
    values = by_block[:, :, None, :] * kernel[:, None, :, :]
    flat_data = values.reshape(blocks, -1)
    moved = jnp.dot(
        select, flat_data, precision=lax.Precision.HIGHEST, preferred_element_type=jnp.float32
    )
    value_buffer = moved.reshape((tiles, CAP) + values.shape[1:])
    payload = lax.all_to_all(value_buffer, "tile", split_axis=0, concat_axis=0, tiled=True)
    cell_index = lax.all_to_all(id_buffer, "tile", split_axis=0, concat_axis=0, tiled=True)

    def single(item_values, item_cells):
        return place_cells(item_values, item_cells, members, levels, rows_x, columns)

    placed = jax.vmap(single, in_axes=(1, 1))(payload, cell_index)
    adjoint = jnp.sum(placed, axis=0).reshape(members, levels, rows_x, columns)
    surface = jnp.zeros((members, rows_x, columns), jnp.float32)
    for repeat in range(STEPS):
        padded = with_halo(adjoint, (("tile", 2),), 1)
        adjoint = advance(padded, wind_x, wind_y, mixing)
        surface = surface + adjoint[:, 0]
    member_total = jnp.sum(surface, axis=0)
    gradient = lax.psum_scatter(member_total, "ens", scatter_dimension=1, tiled=True)
    width = gradient.shape[1]
    first_row = lax.axis_index("tile") * rows_x
    first_col = lax.axis_index("ens") * width
    row_local = sources // NY - first_row
    col_local = sources % NY - first_col
    inside = (row_local >= 0) & (row_local < rows_x) & (col_local >= 0) & (col_local < width)
    values_here = gradient[jnp.clip(row_local, 0, rows_x - 1), jnp.clip(col_local, 0, width - 1)]
    local_pick = jnp.where(inside, values_here, 0.0)
    picked = lax.psum(local_pick, ("tile", "ens"))
    factor = jnp.linalg.cholesky(gram_matrix)
    coefficients = jax.scipy.linalg.cho_solve((factor, True), picked)
    return (gradient, coefficients, adjoint)


def solution(mesh):
    in_specs = (
        P("ens", "tile", None),
        P("tile", None, None),
        P("tile", None),
        P("tile", None),
        P("ens", None, "tile", None),
        P("ens", None, "tile", None),
        P("ens", None, "tile", None),
        P(),
        P(),
    )
    out_specs = (P("tile", "ens"), P(), P("ens", None, "tile", None))
    return jax.shard_map(
        per_device, mesh=mesh, in_specs=in_specs, out_specs=out_specs, check_vma=False
    )
```

profile of v0, /device:TPU:0, one launch (start us, length us, event | category | flops | bytes accessed | tf_op | source)
XLA Modules:
  0.0 157.0 jit_solution(13254592579602345849)
XLA Ops:
  7.2 0.7 fusion.74
  7.9 0.8 select_reduce_fusion.1
  8.8 0.7 multiply_add_fusion.1
  9.4 1.4 multiply_reduce_fusion
  10.8 5.2 %all-to-all-start.1 = ((s32[8,2,128]{2,1,0:T(2,128)}), s32[8,2,128]{2,1,0:T(2,128)S(1)}, u32[]{:S(2)}, u32[]{:S(2)}) async-start(s32[8,2,128]{2,1,0:T(2,128)} %bitcast.8), calls=%async_computation.1 | async-start | bytes 16384 | tf_op jit(solution)/shard_map/all_to_all | solution.py:92
  16.0 0.7 copy.26
  16.7 0.8 multiply_bitcast_fusion
  17.5 0.8 copy.30
  18.2 0.7 fusion.68
  18.9 1.4 cholesky.16
  20.4 0.6 compare_reduce_fusion
  21.1 0.3 fusion.64
  21.4 0.7 fusion.63
  22.1 0.7 copy.27
  22.7 4.2 %all-to-all-start = ((f32[8,2,2,8,128]{4,3,2,1,0:T(8,128)}), f32[8,2,2,8,128]{4,3,2,1,0:T(8,128)S(1)}, u32[]{:S(2)}, u32[]{:S(2)}) async-start(f32[8,2,2,8,128]{4,3,2,1,0:T(8,128)} %copy.27), calls=%async_computation | async-start | bytes 262144 | tf_op jit(solution)/shard_map/all_to_all | solution.py:91
  27.0 5.4 %all-to-all-done = f32[8,2,2,8,128]{4,3,2,1,0:T(8,128)S(1)} async-done(((f32[8,2,2,8,128]{4,3,2,1,0:T(8,128)}), f32[8,2,2,8,128]{4,3,2,1,0:T(8,128)S(1)}, u32[]{:S(2)}, u32[]{:S(2)}) %all-to-all-start) | async-done | bytes 131104 | tf_op jit(solution)/shard_map/all_to_all | solution.py:91
  32.5 0.1 copy.33
  32.6 0.1 reshape.223
  32.6 2.4 %fusion.1 = f32[16,16,512,1]{2,1,3,0:T(8,128)S(1)} fusion(s32[2,1024]{1,0:T(2,128)S(1)} %get-tuple-element.31, f32[2,1024,16]{1,2,0:T(8,128)S(1)} %fusion.61, f32[2,16,1024]{2,0,1:T(2,128)S(1)} %reshape.223), kind=kOutput, calls=%fused_computation.3 | convolution fusion | flops 3222798336 | bytes 794624 | tf_op jit(solution)/shard_map/vmap(arx,ry->axy)/dot_general | solution.py:55
  35.1 0.2 fusion.96
  35.3 0.1 fusion.97
  35.3 1.3 collective-permute-start
  36.7 3.2 %collective-permute-start.1 = (f32[2,8,1,512]{3,2,1,0:T(1,128)S(1)}, f32[2,8,1,512]{3,2,1,0:T(1,128)S(1)}, u32[]{:S(2)}, u32[]{:S(2)}) collective-permute-start(f32[2,8,1,512]{3,2,1,0:T(1,128)S(1)} %get-tuple-element.29), channel_id=1, source_target_pairs={{0,4},{4,8},{8,12},{12,16},{16,20},{20,24},{24,28},{1,5},{5,9},{9,... | collective-permute-start | bytes 98312 | tf_op jit(solution)/shard_map/ppermute | solution.py:18
  39.9 0.1 fusion.60
  40.0 0.7 collective-permute-done.1
  40.7 0.5 fusion.52
  41.2 0.2 fusion.94
  41.4 0.1 fusion.95
  41.5 1.3 collective-permute-start.2
  42.8 3.6 %collective-permute-start.3 = (f32[2,8,1,512]{3,2,1,0:T(1,128)S(1)}, f32[2,8,1,512]{3,2,1,0:T(1,128)S(1)}, u32[]{:S(2)}, u32[]{:S(2)}) collective-permute-start(f32[2,8,1,512]{3,2,1,0:T(1,128)S(1)} %get-tuple-element.25), channel_id=1, source_target_pairs={{0,4},{4,8},{8,12},{12,16},{16,20},{20,24},{24,28},{1,5},{5,9},{9,... | collective-permute-start | bytes 98312 | tf_op jit(solution)/shard_map/ppermute | solution.py:18
  46.4 0.1 fusion.59
  46.5 0.7 collective-permute-done.3
  47.2 0.5 fusion.44
  47.7 0.2 fusion.92
  48.0 1.3 collective-permute-start.4
  49.3 5.0 %collective-permute-start.5 = (f32[2,8,1,512]{3,2,1,0:T(1,128)S(1)}, f32[2,8,1,512]{3,2,1,0:T(1,128)S(1)}, u32[]{:S(2)}, u32[]{:S(2)}) collective-permute-start(f32[2,8,1,512]{3,2,1,0:T(1,128)S(1)} %get-tuple-element.21), channel_id=1, source_target_pairs={{0,4},{4,8},{8,12},{12,16},{16,20},{20,24},{24,28},{1,5},{5,9},{9,... | collective-permute-start | bytes 98312 | tf_op jit(solution)/shard_map/ppermute | solution.py:18
  54.3 0.1 fusion.58
  54.4 0.7 collective-permute-done.5
  55.2 0.5 fusion.36
  55.7 0.2 fusion.90
  55.9 1.3 collective-permute-start.6
  57.2 5.0 %collective-permute-start.7 = (f32[2,8,1,512]{3,2,1,0:T(1,128)S(1)}, f32[2,8,1,512]{3,2,1,0:T(1,128)S(1)}, u32[]{:S(2)}, u32[]{:S(2)}) collective-permute-start(f32[2,8,1,512]{3,2,1,0:T(1,128)S(1)} %get-tuple-element.17), channel_id=1, source_target_pairs={{0,4},{4,8},{8,12},{12,16},{16,20},{20,24},{24,28},{1,5},{5,9},{9,... | collective-permute-start | bytes 98312 | tf_op jit(solution)/shard_map/ppermute | solution.py:18
  62.3 0.1 fusion.57
  62.4 0.7 collective-permute-done.7
  63.1 0.5 fusion.28
  63.6 0.2 fusion.88
  63.9 1.3 collective-permute-start.8
  65.2 5.0 %collective-permute-start.9 = (f32[2,8,1,512]{3,2,1,0:T(1,128)S(1)}, f32[2,8,1,512]{3,2,1,0:T(1,128)S(1)}, u32[]{:S(2)}, u32[]{:S(2)}) collective-permute-start(f32[2,8,1,512]{3,2,1,0:T(1,128)S(1)} %get-tuple-element.13), channel_id=1, source_target_pairs={{0,4},{4,8},{8,12},{12,16},{16,20},{20,24},{24,28},{1,5},{5,9},{9,... | collective-permute-start | bytes 98312 | tf_op jit(solution)/shard_map/ppermute | solution.py:18
  70.2 0.1 fusion.56
  70.3 0.7 collective-permute-done.9
  71.1 0.5 fusion.20
  71.6 0.2 fusion.86
  71.9 1.3 collective-permute-start.10
  73.2 5.0 %collective-permute-start.11 = (f32[2,8,1,512]{3,2,1,0:T(1,128)S(1)}, f32[2,8,1,512]{3,2,1,0:T(1,128)S(1)}, u32[]{:S(2)}, u32[]{:S(2)}) collective-permute-start(f32[2,8,1,512]{3,2,1,0:T(1,128)S(1)} %get-tuple-element.9), channel_id=1, source_target_pairs={{0,4},{4,8},{8,12},{12,16},{16,20},{20,24},{24,28},{1,5},{5,9},{9,... | collective-permute-start | bytes 98312 | tf_op jit(solution)/shard_map/ppermute | solution.py:18
  78.2 0.1 fusion.55
  78.3 0.7 collective-permute-done.11
  79.0 0.5 fusion.12
  79.6 0.7 fusion.62
  80.3 28.0 %reduce-scatter.2.cloned.1.call-done = f32[16,128]{1,0:T(8,128)} async-done(((f32[16,512]{1,0:T(8,128)}), f32[16,128]{1,0:T(8,128)}) %reduce-scatter.2.cloned.1.call-update) | async-done | bytes 8208 | tf_op jit(solution)/shard_map/reduce_scatter | solution.py:105
  108.3 1.4 gather_fusion
  109.7 1.2 custom-call.10
  110.9 38.4 %psum.7 = f32[16]{0:T(128)S(1)} all-reduce(f32[16]{0:T(128)S(1)} %and_select_fusion.2), channel_id=1, replica_groups=mesh['tile'=8,'ens'=4] {'tile','ens'}, use_global_device_ids=true, to_apply=%region_7.8 | all-reduce | flops 16 | bytes 128 | tf_op jit(solution)/shard_map/psum | solution.py:114
  149.3 0.1 convolution_bitcast_fusion.1
  149.5 0.7 convolution_bitcast_fusion
  (32 shorter events, 0.5 us)
Async XLA Ops:
  10.8 11.9 %all-to-all-start.1 = ((s32[8,2,128]{2,1,0:T(2,128)}), s32[8,2,128]{2,1,0:T(2,128)S(1)}, u32[]{:S(2)}, u32[]{:S(2)}) async-start(s32[8,2,128]{2,1,0:T(2,128)} %bitcast.8), calls=%async_computation.1 | async-start | bytes 16384 | tf_op jit(solution)/shard_map/all_to_all | solution.py:92
  22.7 9.7 %all-to-all-start = ((f32[8,2,2,8,128]{4,3,2,1,0:T(8,128)}), f32[8,2,2,8,128]{4,3,2,1,0:T(8,128)S(1)}, u32[]{:S(2)}, u32[]{:S(2)}) async-start(f32[8,2,2,8,128]{4,3,2,1,0:T(8,128)} %copy.27), calls=%async_computation | async-start | bytes 262144 | tf_op jit(solution)/shard_map/all_to_all | solution.py:91
  26.9 81.4 %reduce-scatter.2.cloned.1.call-start = ((), (), s32[]{:S(2)}) async-start(), calls=%async_computation.3 | async-start | bytes 40960 | tf_op jit(solution)/shard_map/reduce_scatter | solution.py:105
  35.1 4.8 %copy-start.2 = (f32[2,8,16,512]{3,2,1,0:T(8,128)S(1)}, f32[2,8,16,512]{3,2,1,0:T(8,128)}, u32[]{:S(2)}) copy-start(f32[2,8,16,512]{3,2,1,0:T(8,128)} %param.15) | copy-start | bytes 1572868
  35.3 4.6 %collective-permute-start = (f32[2,8,1,512]{3,2,1,0:T(1,128)S(1)}, f32[2,8,1,512]{3,2,1,0:T(1,128)S(1)}, u32[]{:S(2)}, u32[]{:S(2)}) collective-permute-start(f32[2,8,1,512]{3,2,1,0:T(1,128)S(1)} %get-tuple-element.28), channel_id=1, source_target_pairs={{4,0},{8,4},{12,8},{16,12},{20,16},{24,20},{28,24},{5,1},{9,5},{13... | collective-permute-start | bytes 98312 | tf_op jit(solution)/shard_map/ppermute | solution.py:19
  36.6 4.0 %copy-start = (f32[2,8,16,512]{3,2,1,0:T(8,128)S(1)}, f32[2,8,16,512]{3,2,1,0:T(8,128)}, u32[]{:S(2)}) copy-start(f32[2,8,16,512]{3,2,1,0:T(8,128)} %param.14) | copy-start | bytes 1572868
  36.7 4.0 %copy-start.1 = (f32[2,8,16,512]{3,2,1,0:T(8,128)S(1)}, f32[2,8,16,512]{3,2,1,0:T(8,128)}, u32[]{:S(2)}) copy-start(f32[2,8,16,512]{3,2,1,0:T(8,128)} %param.13) | copy-start | bytes 1572868
  36.7 4.0 %collective-permute-start.1 = (f32[2,8,1,512]{3,2,1,0:T(1,128)S(1)}, f32[2,8,1,512]{3,2,1,0:T(1,128)S(1)}, u32[]{:S(2)}, u32[]{:S(2)}) collective-permute-start(f32[2,8,1,512]{3,2,1,0:T(1,128)S(1)} %get-tuple-element.29), channel_id=1, source_target_pairs={{0,4},{4,8},{8,12},{12,16},{16,20},{20,24},{24,28},{1,5},{5,9},{9,... | collective-permute-start | bytes 98312 | tf_op jit(solution)/shard_map/ppermute | solution.py:18
  41.5 5.0 %collective-permute-start.2 = (f32[2,8,1,512]{3,2,1,0:T(1,128)S(1)}, f32[2,8,1,512]{3,2,1,0:T(1,128)S(1)}, u32[]{:S(2)}, u32[]{:S(2)}) collective-permute-start(f32[2,8,1,512]{3,2,1,0:T(1,128)S(1)} %get-tuple-element.24), channel_id=1, source_target_pairs={{4,0},{8,4},{12,8},{16,12},{20,16},{24,20},{28,24},{5,1},{9,5},{13... | collective-permute-start | bytes 98312 | tf_op jit(solution)/shard_map/ppermute | solution.py:19
  42.8 4.4 %collective-permute-start.3 = (f32[2,8,1,512]{3,2,1,0:T(1,128)S(1)}, f32[2,8,1,512]{3,2,1,0:T(1,128)S(1)}, u32[]{:S(2)}, u32[]{:S(2)}) collective-permute-start(f32[2,8,1,512]{3,2,1,0:T(1,128)S(1)} %get-tuple-element.25), channel_id=1, source_target_pairs={{0,4},{4,8},{8,12},{12,16},{16,20},{20,24},{24,28},{1,5},{5,9},{9,... | collective-permute-start | bytes 98312 | tf_op jit(solution)/shard_map/ppermute | solution.py:18
  48.0 6.4 %collective-permute-start.4 = (f32[2,8,1,512]{3,2,1,0:T(1,128)S(1)}, f32[2,8,1,512]{3,2,1,0:T(1,128)S(1)}, u32[]{:S(2)}, u32[]{:S(2)}) collective-permute-start(f32[2,8,1,512]{3,2,1,0:T(1,128)S(1)} %get-tuple-element.20), channel_id=1, source_target_pairs={{4,0},{8,4},{12,8},{16,12},{20,16},{24,20},{28,24},{5,1},{9,5},{13... | collective-permute-start | bytes 98312 | tf_op jit(solution)/shard_map/ppermute | solution.py:19
  49.3 5.9 %collective-permute-start.5 = (f32[2,8,1,512]{3,2,1,0:T(1,128)S(1)}, f32[2,8,1,512]{3,2,1,0:T(1,128)S(1)}, u32[]{:S(2)}, u32[]{:S(2)}) collective-permute-start(f32[2,8,1,512]{3,2,1,0:T(1,128)S(1)} %get-tuple-element.21), channel_id=1, source_target_pairs={{0,4},{4,8},{8,12},{12,16},{16,20},{20,24},{24,28},{1,5},{5,9},{9,... | collective-permute-start | bytes 98312 | tf_op jit(solution)/shard_map/ppermute | solution.py:18
  55.9 6.4 %collective-permute-start.6 = (f32[2,8,1,512]{3,2,1,0:T(1,128)S(1)}, f32[2,8,1,512]{3,2,1,0:T(1,128)S(1)}, u32[]{:S(2)}, u32[]{:S(2)}) collective-permute-start(f32[2,8,1,512]{3,2,1,0:T(1,128)S(1)} %get-tuple-element.16), channel_id=1, source_target_pairs={{4,0},{8,4},{12,8},{16,12},{20,16},{24,20},{28,24},{5,1},{9,5},{13... | collective-permute-start | bytes 98312 | tf_op jit(solution)/shard_map/ppermute | solution.py:19
  57.2 5.9 %collective-permute-start.7 = (f32[2,8,1,512]{3,2,1,0:T(1,128)S(1)}, f32[2,8,1,512]{3,2,1,0:T(1,128)S(1)}, u32[]{:S(2)}, u32[]{:S(2)}) collective-permute-start(f32[2,8,1,512]{3,2,1,0:T(1,128)S(1)} %get-tuple-element.17), channel_id=1, source_target_pairs={{0,4},{4,8},{8,12},{12,16},{16,20},{20,24},{24,28},{1,5},{5,9},{9,... | collective-permute-start | bytes 98312 | tf_op jit(solution)/shard_map/ppermute | solution.py:18
  63.9 6.4 %collective-permute-start.8 = (f32[2,8,1,512]{3,2,1,0:T(1,128)S(1)}, f32[2,8,1,512]{3,2,1,0:T(1,128)S(1)}, u32[]{:S(2)}, u32[]{:S(2)}) collective-permute-start(f32[2,8,1,512]{3,2,1,0:T(1,128)S(1)} %get-tuple-element.12), channel_id=1, source_target_pairs={{4,0},{8,4},{12,8},{16,12},{20,16},{24,20},{28,24},{5,1},{9,5},{13... | collective-permute-start | bytes 98312 | tf_op jit(solution)/shard_map/ppermute | solution.py:19
  65.2 5.9 %collective-permute-start.9 = (f32[2,8,1,512]{3,2,1,0:T(1,128)S(1)}, f32[2,8,1,512]{3,2,1,0:T(1,128)S(1)}, u32[]{:S(2)}, u32[]{:S(2)}) collective-permute-start(f32[2,8,1,512]{3,2,1,0:T(1,128)S(1)} %get-tuple-element.13), channel_id=1, source_target_pairs={{0,4},{4,8},{8,12},{12,16},{16,20},{20,24},{24,28},{1,5},{5,9},{9,... | collective-permute-start | bytes 98312 | tf_op jit(solution)/shard_map/ppermute | solution.py:18
  71.9 6.4 %collective-permute-start.10 = (f32[2,8,1,512]{3,2,1,0:T(1,128)S(1)}, f32[2,8,1,512]{3,2,1,0:T(1,128)S(1)}, u32[]{:S(2)}, u32[]{:S(2)}) collective-permute-start(f32[2,8,1,512]{3,2,1,0:T(1,128)S(1)} %get-tuple-element.8), channel_id=1, source_target_pairs={{4,0},{8,4},{12,8},{16,12},{20,16},{24,20},{28,24},{5,1},{9,5},{13... | collective-permute-start | bytes 98312 | tf_op jit(solution)/shard_map/ppermute | solution.py:19
  73.2 5.9 %collective-permute-start.11 = (f32[2,8,1,512]{3,2,1,0:T(1,128)S(1)}, f32[2,8,1,512]{3,2,1,0:T(1,128)S(1)}, u32[]{:S(2)}, u32[]{:S(2)}) collective-permute-start(f32[2,8,1,512]{3,2,1,0:T(1,128)S(1)} %get-tuple-element.9), channel_id=1, source_target_pairs={{0,4},{4,8},{8,12},{12,16},{16,20},{20,24},{24,28},{1,5},{5,9},{9,... | collective-permute-start | bytes 98312 | tf_op jit(solution)/shard_map/ppermute | solution.py:18
  79.0 1.3 copy-start.4
  79.5 70.6 %copy-start.3 = (f32[2,8,16,512]{3,2,1,0:T(8,128)}, f32[2,8,16,512]{3,2,1,0:T(8,128)S(1)}, u32[]{:S(2)}) copy-start(f32[2,8,16,512]{3,2,1,0:T(8,128)S(1)} %fusion.12) | copy-start | bytes 1572868
Sparse Core Ops, SparseCore 0:
  80.4 27.8 reduce-scatter.1
where the time goes:
time: 158 us; the launch traced here: 157 us
  starting transfers between devices  43.9 us (28%)
  blocking collectives  38.4 us (24%)
  waiting for transfers between devices  37.9 us (24%)
  between operations  14.4 us (9%)
  other arithmetic  13.5 us (9%)
  local copies, waits for them, and re-layouts  5.3 us (3%)
  matrix products  3.52 us (2%)
    psum x1, blocking collectives, per_device(): picked = lax.psum(local_pick, ('tile', 'ens'))  38.4 us
    reduce_scatter x1, waiting for transfers between devices, per_device(): lax.psum_scatter(member_total, 'ens', scatter_dimension=1, tiled=True)  28 us
    ppermute x6, starting transfers between devices, with_halo(): before = lax.ppermute(last, axis, up)  26.8 us
    ppermute x6, starting transfers between devices, with_halo(): after = lax.ppermute(initial, axis, down)  7.75 us
    all_to_all x1, waiting for transfers between devices, per_device(): lax.all_to_all(value_buffer, 'tile', split_axis=0, concat_axis=0, tiled=T...  5.43 us
    all_to_all x1, starting transfers between devices, per_device(): lax.all_to_all(id_buffer, 'tile', split_axis=0, concat_axis=0, tiled=True)  5.17 us
    ppermute x6, waiting for transfers between devices, with_halo(): before = lax.ppermute(last, axis, up)  4.42 us
    all_to_all x1, starting transfers between devices, per_device(): lax.all_to_all(value_buffer, 'tile', split_axis=0, concat_axis=0, tiled=T...  4.2 us
  transfers between devices with their start and end apart: 15, of which 8 were waited for; matrix products, arithmetic and copies ran while one was open for 5% of the time, Pallas kernels for 0%

commit v1 on v0

v1 whole, which is shorter than its diff:
```python
import functools

import jax
import jax.numpy as jnp
from jax import lax
from jax.experimental import pallas as pl
from jax.experimental.pallas import tpu as pltpu
from jax.sharding import PartitionSpec as P

CAP = 2
STEPS = 6
HALO = 2
GROUP = 8
LANES = 128


def roll(array, shift, axis):
    return pltpu.roll(array, shift % array.shape[axis], axis=axis)


def body(
    dims,
    dest_ref,
    sources_ref,
    residual_ref,
    kernel_ref,
    cells_ref,
    gram_ref,
    wx_ref,
    wy_ref,
    mix_ref,
    grad_ref,
    coef_ref,
    adj_ref,
    raw,
    coefs,
    states,
    total,
    outbuf,
    send_obs,
    recv_obs,
    left_hi,
    left_lo,
    right_hot,
    forcing,
    level0,
    picks,
    send_sum,
    recv_sum,
    send_pick,
    recv_pick,
    augmented,
    local_sem,
    obs_send,
    obs_recv,
    edge_send,
    edge_recv,
    halo_send,
    halo_recv,
    sum_send,
    sum_recv,
    pick_send,
    pick_recv,
    out_sem,
):
    tiles, groups, members, levels, rows, columns, blocks = dims
    width = columns // groups
    strips = columns // LANES
    nsrc = gram_ref.shape[0]
    me = lax.axis_index("tile")
    mine = lax.axis_index("ens")
    depth = members * levels
    log_columns = columns.bit_length() - 1

    loads = []
    for which, source in enumerate((wx_ref, wy_ref, mix_ref)):
        for j in range(strips):
            copy = pltpu.make_async_copy(
                source.at[:, pl.ds(j * LANES, LANES)],
                raw.at[which, j],
                local_sem.at[which, j],
            )
            copy.start()
            loads.append(copy)

    barrier = pltpu.get_barrier_semaphore()

    def greet_tile(d, carry):
        peer = lax.rem(me + d, tiles)
        pl.semaphore_signal(barrier, inc=1, device_id={"tile": peer})
        return carry

    def greet_ens(d, carry):
        peer = lax.rem(mine + d, groups)
        pl.semaphore_signal(barrier, inc=1, device_id={"ens": peer})
        return carry

    lax.fori_loop(1, tiles, greet_tile, 0)
    lax.fori_loop(1, groups, greet_ens, 0)

    def fill(tile, carry):
        def look(b, found):
            first, second = found
            here = dest_ref[b, 0] == tile
            second = jnp.where(here & (first >= 0) & (second < 0), b, second)
            first = jnp.where(here & (first < 0), b, first)
            return first, second

        none = jnp.int32(-1)
        found = lax.fori_loop(0, blocks, look, (none, none), unroll=min(blocks, 8))
        for c in range(CAP):
            block = jnp.maximum(found[c], 0)
            held = found[c] >= 0
            send_obs[tile, c * levels : (c + 1) * levels, :] = kernel_ref[block]
            base = CAP * levels + c * (members + 2)
            for m in range(members):
                part = residual_ref[m, pl.ds(block, 1), :]
                send_obs[tile, base + m : base + m + 1, :] = jnp.where(held, part, 0.0)
            ids = cells_ref[pl.ds(block, 1), :].astype(jnp.float32)
            send_obs[tile, base + members : base + members + 1, :] = ids
        return carry

    lax.fori_loop(0, tiles, fill, 0)

    pl.semaphore_wait(barrier, tiles + groups - 2)

    def obs_copy(d):
        peer = lax.rem(me + d, tiles)
        return pltpu.make_async_remote_copy(
            src_ref=send_obs.at[peer],
            dst_ref=recv_obs.at[me],
            send_sem=obs_send.at[d],
            recv_sem=obs_recv.at[d],
            device_id={"tile": peer},
        )

    def start_obs(d, carry):
        obs_copy(d).start()
        return carry

    lax.fori_loop(1, tiles, start_obs, 0)
    recv_obs[me] = send_obs[me]

    for t in range(0, STEPS + 1):

        @pl.when(me == 0)
        def _():
            states[t, 0:HALO] = jnp.zeros((HALO, members, levels, columns), jnp.float32)

        @pl.when(me == tiles - 1)
        def _():
            states[t, HALO + rows :] = jnp.zeros((HALO, members, levels, columns), jnp.float32)

    edge = HALO - 1
    if edge:

        @pl.when(me == 0)
        def _():
            coefs[0:edge] = jnp.zeros((edge,) + coefs.shape[1:], jnp.float32)

        @pl.when(me == tiles - 1)
        def _():
            coefs[edge + rows :] = jnp.zeros((edge,) + coefs.shape[1:], jnp.float32)

    for copy in loads:
        copy.wait()

    level_iota = lax.broadcasted_iota(jnp.int32, (levels, LANES), 0)
    lane_iota = lax.broadcasted_iota(jnp.int32, (levels, LANES), 1)

    def prepare(x, carry):
        for m in range(members):
            at = pl.ds(m * levels * rows + x, levels, stride=rows)
            for j in range(strips):
                wx = raw[0, j, at, :]
                wy = raw[1, j, at, :]
                mixing = raw[2, j, at, :]
                center = 1.0 - jnp.abs(wx) - jnp.abs(wy)
                if j == 0:
                    wy = jnp.where((lane_iota == 0) & (wy < 0.0), 0.0, wy)
                if j == strips - 1:
                    wy = jnp.where((lane_iota == LANES - 1) & (wy > 0.0), 0.0, wy)
                mixing = jnp.where(level_iota == levels - 1, 0.0, mixing)
                lanes = slice(j * LANES, (j + 1) * LANES)
                coefs[edge + x, 0, m, :, lanes] = center
                coefs[edge + x, 1, m, :, lanes] = wx
                coefs[edge + x, 2, m, :, lanes] = wy
                coefs[edge + x, 3, m, :, lanes] = mixing
        return carry

    lax.fori_loop(0, rows, prepare, 0)

    def edge_copy(upward):
        if upward:
            return pltpu.make_async_remote_copy(
                src_ref=coefs.at[pl.ds(rows, edge)],
                dst_ref=coefs.at[pl.ds(0, edge)],
                send_sem=edge_send.at[0],
                recv_sem=edge_recv.at[0],
                device_id={"tile": me + 1},
            )
        return pltpu.make_async_remote_copy(
            src_ref=coefs.at[pl.ds(edge, edge)],
            dst_ref=coefs.at[pl.ds(edge + rows, edge)],
            send_sem=edge_send.at[1],
            recv_sem=edge_recv.at[1],
            device_id={"tile": me - 1},
        )

    def halo_copy(t, upward):
        n = t // HALO
        if upward:
            return pltpu.make_async_remote_copy(
                src_ref=states.at[t, pl.ds(rows, HALO)],
                dst_ref=states.at[t, pl.ds(0, HALO)],
                send_sem=halo_send.at[0, n],
                recv_sem=halo_recv.at[0, n],
                device_id={"tile": me + 1},
            )
        return pltpu.make_async_remote_copy(
            src_ref=states.at[t, pl.ds(HALO, HALO)],
            dst_ref=states.at[t, pl.ds(HALO + rows, HALO)],
            send_sem=halo_send.at[1, n],
            recv_sem=halo_recv.at[1, n],
            device_id={"tile": me - 1},
        )

    def start_both(make):
        @pl.when(me < tiles - 1)
        def _():
            make(True).start()

        @pl.when(me > 0)
        def _():
            make(False).start()

    def await_both(make):
        @pl.when(me > 0)
        def _():
            make(True).wait_recv()

        @pl.when(me < tiles - 1)
        def _():
            make(False).wait_recv()

    def drain_both(make):
        @pl.when(me < tiles - 1)
        def _():
            make(True).wait_send()

        @pl.when(me > 0)
        def _():
            make(False).wait_send()

    if edge:
        start_both(edge_copy)

    row_iota = lax.broadcasted_iota(jnp.int32, (nsrc, LANES), 0)
    col_iota = lax.broadcasted_iota(jnp.int32, (nsrc, LANES), 1)
    augmented[...] = jnp.where(row_iota == col_iota, 1.0, 0.0)
    augmented[:, nsrc : 2 * nsrc] = gram_ref[...]
    table = augmented[...]
    for i in range(nsrc):
        pivot = table[i : i + 1, :]
        scaled = pivot / table[i : i + 1, nsrc + i : nsrc + i + 1]
        column = table[:, nsrc + i : nsrc + i + 1]
        table = jnp.where(row_iota == i, scaled, table - column * scaled)
    augmented[...] = table

    def await_obs(d, carry):
        obs_copy(d).wait()
        return carry

    lax.fori_loop(1, tiles, await_obs, 0)

    group = min(GROUP, tiles)
    part_rows = LANES * CAP
    cell_rows = lax.broadcasted_iota(jnp.int32, (rows, depth, LANES), 0)
    cell_cols = lax.broadcasted_iota(jnp.int32, (columns, LANES), 0)

    def place(g, carry):
        for s in range(group):
            block = recv_obs[g * group + s]
            for c in range(CAP):
                at = s * part_rows + c * LANES
                base = CAP * levels + c * (members + 2)
                weights = block[c * levels : (c + 1) * levels]
                values = jnp.concatenate(
                    [weights * block[base + m : base + m + 1] for m in range(members)], axis=0
                )
                ids = block[base + members : base + members + 1].astype(jnp.int32)
                row = jnp.right_shift(ids, log_columns)
                col = jnp.bitwise_and(ids, columns - 1)
                high = values.astype(jnp.bfloat16).astype(jnp.float32)
                low = values - high
                inside = cell_rows == row[None]
                shape = (rows * depth, LANES)
                left_hi[:, at : at + LANES] = (
                    jnp.where(inside, high[None], 0.0).reshape(shape).astype(jnp.bfloat16)
                )
                left_lo[:, at : at + LANES] = (
                    jnp.where(inside, low[None], 0.0).reshape(shape).astype(jnp.bfloat16)
                )
                right_hot[:, at : at + LANES] = jnp.where(cell_cols == col, 1.0, 0.0).astype(
                    jnp.bfloat16
                )
        numbers = (((1,), (1,)), ((), ()))
        hot = right_hot[...]
        placed = lax.dot_general(left_hi[...], hot, numbers, preferred_element_type=jnp.float32)
        placed += lax.dot_general(left_lo[...], hot, numbers, preferred_element_type=jnp.float32)
        if group == tiles:
            forcing[...] = placed
        else:
            forcing[...] += placed
        return carry

    if group == tiles:
        place(0, 0)
    else:
        forcing[...] = jnp.zeros_like(forcing)
        lax.fori_loop(0, tiles // group, place, 0)
    states[0, HALO : HALO + rows] = forcing[...].reshape(rows, members, levels, columns)

    for t in range(STEPS):
        part = t % HALO
        if part == 0:
            start_both(functools.partial(halo_copy, t))
            if t == 0 and edge:
                await_both(edge_copy)
            await_both(functools.partial(halo_copy, t))
        reach = HALO - 1 - part
        last = t == STEPS - 1

        def advance(r, carry):
            summed = None
            for m in range(members):
                here = states[t, r, m]
                above = states[t, r + 1, m]
                below = states[t, r - 1, m]
                center = coefs[r - 1, 0, m]
                wx = coefs[r - 1, 1, m]
                wy = coefs[r - 1, 2, m]
                mixing = coefs[r - 1, 3, m]
                right = roll(here, -1, 1)
                left = roll(here, 1, 1)
                flux = mixing * (roll(here, -1, 0) - here)
                new = center * here
                new += jnp.abs(wx) * jnp.where(wx > 0.0, above, below)
                new += jnp.abs(wy) * jnp.where(wy > 0.0, right, left)
                new += flux - roll(flux, 1, 0)
                if last:
                    at = pl.ds(m * levels * rows + r - HALO, levels, stride=rows)
                    for j in range(strips):
                        outbuf[j, at, :] = new[:, j * LANES : (j + 1) * LANES]
                else:
                    states[t + 1, r, m] = new
                summed = new if summed is None else summed + new
            if t > 0:
                summed = summed + total[r]
            total[r] = summed
            return carry

        lax.fori_loop(HALO - reach, HALO + rows + reach, advance, 0)

    stores = []
    for j in range(strips):
        copy = pltpu.make_async_copy(
            outbuf.at[j], adj_ref.at[:, pl.ds(j * LANES, LANES)], out_sem.at[j]
        )
        copy.start()
        stores.append(copy)

    for x in range(rows):
        level0[x : x + 1, :] = total[HALO + x, 0:1, :]
    for e in range(groups):
        send_sum[e, 0:rows, :] = level0[:, e * width : (e + 1) * width]
    wide_iota = lax.broadcasted_iota(jnp.int32, (1, columns), 1)
    for s in range(nsrc):
        place_of = sources_ref[s]
        row = jnp.right_shift(place_of, log_columns) - me * rows
        col = jnp.bitwise_and(place_of, columns - 1)
        inside = (row >= 0) & (row < rows)
        line = level0[pl.ds(jnp.clip(row, 0, rows - 1), 1), :]
        picks[s : s + 1, :] = jnp.where(wide_iota == jnp.where(inside, col, -1), line, 0.0)
    found = jnp.sum(picks[...], axis=1, keepdims=True)
    found = jnp.broadcast_to(found, (nsrc, width))
    for e in range(groups):
        send_sum[e, rows : rows + nsrc, :] = found

    def sum_copy(d):
        peer = lax.rem(mine + d, groups)
        return pltpu.make_async_remote_copy(
            src_ref=send_sum.at[peer],
            dst_ref=recv_sum.at[mine],
            send_sem=sum_send.at[d],
            recv_sem=sum_recv.at[d],
            device_id={"ens": peer},
        )

    for d in range(1, groups):
        sum_copy(d).start()
    recv_sum[mine] = send_sum[mine]
    for d in range(1, groups):
        sum_copy(d).wait()
    summed = recv_sum[0]
    for e in range(1, groups):
        summed = summed + recv_sum[e]
    grad_ref[...] = summed[0:rows]
    send_pick[...] = summed[rows : rows + nsrc]

    def pick_copy(d):
        peer = lax.rem(me + d, tiles)
        return pltpu.make_async_remote_copy(
            src_ref=send_pick,
            dst_ref=recv_pick.at[me],
            send_sem=pick_send.at[d],
            recv_sem=pick_recv.at[d],
            device_id={"tile": peer},
        )

    def start_pick(d, carry):
        pick_copy(d).start()
        return carry

    def await_pick(d, carry):
        pick_copy(d).wait()
        return carry

    lax.fori_loop(1, tiles, start_pick, 0)
    recv_pick[me] = send_pick[...]

    if edge:
        drain_both(edge_copy)
    for t in range(0, STEPS, HALO):
        drain_both(functools.partial(halo_copy, t))
    for copy in stores:
        copy.wait()

    lax.fori_loop(1, tiles, await_pick, 0)

    def gather(i, picked):
        return picked + recv_pick[i]

    picked = lax.fori_loop(1, tiles, gather, recv_pick[0])
    solved = jnp.sum(augmented[...] * picked, axis=0, keepdims=True)
    coef_ref[...] = solved[:, 0:nsrc]


def per_device(residual, kernel, dest_tile, cell_ids, wind_x, wind_y, mixing, sources, gram_matrix):
    tiles, groups = lax.axis_size("tile"), lax.axis_size("ens")
    members, levels, rows, columns = wind_x.shape
    blocks = cell_ids.shape[0]
    nsrc = gram_matrix.shape[0]
    strips = columns // LANES
    width = columns // groups
    flat = (members * levels * rows, columns)
    dims = (tiles, groups, members, levels, rows, columns, blocks)
    edge_rows = rows + 2 * (HALO - 1)
    state_rows = rows + 2 * HALO
    rounds = -(-STEPS // HALO)
    obs_rows = CAP * (levels + members + 2)
    span = min(GROUP, tiles) * CAP * LANES
    smem = pl.BlockSpec(memory_space=pltpu.SMEM)
    vmem = pl.BlockSpec(memory_space=pltpu.VMEM)
    anywhere = pl.BlockSpec(memory_space=pl.ANY)
    f32, bf16 = jnp.float32, jnp.bfloat16
    dma = pltpu.SemaphoreType.DMA
    gradient, coefficients, adjoint = pl.pallas_call(
        functools.partial(body, dims),
        out_shape=(
            jax.ShapeDtypeStruct((rows, width), f32),
            jax.ShapeDtypeStruct((1, nsrc), f32),
            jax.ShapeDtypeStruct(flat, f32),
        ),
        in_specs=[smem, smem, vmem, vmem, vmem, vmem, anywhere, anywhere, anywhere],
        out_specs=(vmem, vmem, anywhere),
        scratch_shapes=[
            pltpu.VMEM((3, strips, flat[0], LANES), f32),
            pltpu.VMEM((edge_rows, 4, members, levels, columns), f32),
            pltpu.VMEM((STEPS + 1, state_rows, members, levels, columns), f32),
            pltpu.VMEM((state_rows, levels, columns), f32),
            pltpu.VMEM((strips, flat[0], LANES), f32),
            pltpu.VMEM((tiles, obs_rows, LANES), f32),
            pltpu.VMEM((tiles, obs_rows, LANES), f32),
            pltpu.VMEM((rows * members * levels, span), bf16),
            pltpu.VMEM((rows * members * levels, span), bf16),
            pltpu.VMEM((columns, span), bf16),
            pltpu.VMEM((rows * members * levels, columns), f32),
            pltpu.VMEM((rows, columns), f32),
            pltpu.VMEM((nsrc, columns), f32),
            pltpu.VMEM((groups, rows + nsrc, width), f32),
            pltpu.VMEM((groups, rows + nsrc, width), f32),
            pltpu.VMEM((nsrc, width), f32),
            pltpu.VMEM((tiles, nsrc, width), f32),
            pltpu.VMEM((nsrc, LANES), f32),
            dma((3, strips)),
            dma((tiles,)),
            dma((tiles,)),
            dma((2,)),
            dma((2,)),
            dma((2, rounds)),
            dma((2, rounds)),
            dma((groups,)),
            dma((groups,)),
            dma((tiles,)),
            dma((tiles,)),
            dma((strips,)),
        ],
        compiler_params=pltpu.CompilerParams(
            collective_id=0, has_side_effects=True, vmem_limit_bytes=40 * 1024 * 1024
        ),
        cost_estimate=pl.CostEstimate(
            flops=1_000_000_000, bytes_accessed=2_200_000, transcendentals=0
        ),
    )(
        dest_tile,
        sources,
        residual,
        kernel,
        cell_ids,
        gram_matrix,
        wind_x.reshape(flat),
        wind_y.reshape(flat),
        mixing.reshape(flat),
    )
    return gradient, coefficients.reshape(nsrc), adjoint.reshape(wind_x.shape)


def solution(mesh):
    in_specs = (
        P("ens", "tile", None),
        P("tile", None, None),
        P("tile", None),
        P("tile", None),
        P("ens", None, "tile", None),
        P("ens", None, "tile", None),
        P("ens", None, "tile", None),
        P(),
        P(),
    )
    out_specs = (P("tile", "ens"), P(), P("ens", None, "tile", None))
    return jax.shard_map(
        per_device, mesh=mesh, in_specs=in_specs, out_specs=out_specs, check_vma=False
    )
```

time: 158 us -> 47.3 us (0.30)
  starting transfers between devices: 43.9 us -> 0 us
  blocking collectives: 38.4 us -> 0 us
  Pallas kernels: 0 us -> 38.3 us
  waiting for transfers between devices: 37.9 us -> 0 us
  between operations: 14.4 us -> 0.66 us
  other arithmetic: 13.5 us -> 0 us
  matrix products: 3.52 us -> 0 us
  local copies, waits for them, and re-layouts: 5.3 us -> 7.92 us
    psum x1 -> x0, blocking collectives: 38.4 us -> none  [per_device(): picked = lax.psum(local_pick, ('tile', 'ens'))]
    pallas_call x0 -> x1, Pallas kernels: none -> 38.3 us  [per_device(): pl.pallas_call(functools.partial(body, dims), out_shape=(jax.ShapeDtypeSt...]
    ppermute x12 -> x0, starting transfers between devices: 34.5 us -> none  [the longest x6 26.8 us: with_halo(): before = lax.ppermute(last, axis, up)]
    reduce_scatter x1 -> x0, waiting for transfers between devices: 28 us -> none  [per_device(): lax.psum_scatter(member_total, 'ens', scatter_dimension=1, tiled=True)]
    all_to_all x2 -> x0, starting transfers between devices: 9.37 us -> none  [the longest x1 5.17 us: per_device(): lax.all_to_all(id_buffer, 'tile', split_axis=0, concat_axis=0, tiled=True)]
    unnamed x12 -> x20, local copies, waits for them, and re-layouts: 0.82 us -> 7.92 us
    all_to_all x2 -> x0, waiting for transfers between devices: 5.43 us -> none  [the longest x1 5.43 us: per_device(): lax.all_to_all(value_buffer, 'tile', split_axis=0, concat_axis=0, tiled=T...]
    ppermute x12 -> x0, waiting for transfers between devices: 4.43 us -> none  [the longest x6 4.42 us: with_halo(): before = lax.ppermute(last, axis, up)]
  transfers between devices with their start and end apart: 15 -> 0, of which waited for: 8 -> 0; matrix products, arithmetic and copies ran while one was open for 5% -> 0% of each run, Pallas kernels for 0% -> 0%
where the time goes in v1:
time: 47.3 us; the launch traced here: 46.9 us
  Pallas kernels  38.3 us (81%)
  local copies, waits for them, and re-layouts  7.92 us (17%)
  between operations  0.66 us (1%)
    pallas_call x1, Pallas kernels, per_device(): pl.pallas_call(functools.partial(body, dims), out_shape=(jax.ShapeDtypeSt...  38.3 us
    unnamed x20, local copies, waits for them, and re-layouts  7.92 us

profile of v1, /device:TPU:0, one launch (start us, length us, event | category | flops | bytes accessed | tf_op | source)
XLA Modules:
  0.0 46.9 jit_solution(9624835060799967790)
XLA Ops:
  0.6 0.0 copy-start.4
  0.6 0.0 copy-start.7
  0.7 0.7 %copy.12.dest_ref = s32[8,1]{1,0:T(8,128)S(1)} copy(s32[8,1]{0,1:T(1,128)} %param.11) | data formatting | bytes 64 | tf_op args[2]
  1.4 0.0 copy-done.4
  1.4 0.0 copy-done.7
  1.4 0.0 copy-start
  1.4 1.0 %copy-done = f32[2,8,16,512]{3,2,1,0:T(8,128)S(1)} copy-done((f32[2,8,16,512]{3,2,1,0:T(8,128)S(1)}, f32[2,8,16,512]{3,2,1,0:T(8,128)}, u32[]{:S(2)}) %copy-start) | copy-done | bytes 524312
  2.4 0.0 copy-start.1
  2.4 1.0 %copy-done.1 = f32[2,8,16,512]{3,2,1,0:T(8,128)S(1)} copy-done((f32[2,8,16,512]{3,2,1,0:T(8,128)S(1)}, f32[2,8,16,512]{3,2,1,0:T(8,128)}, u32[]{:S(2)}) %copy-start.1) | copy-done | bytes 524312
  3.5 0.0 copy-start.2
  3.5 1.0 %copy-done.2 = f32[2,8,16,512]{3,2,1,0:T(8,128)S(1)} copy-done((f32[2,8,16,512]{3,2,1,0:T(8,128)S(1)}, f32[2,8,16,512]{3,2,1,0:T(8,128)}, u32[]{:S(2)}) %copy-start.2) | copy-done | bytes 524312
  4.5 0.0 copy-start.3
  4.5 0.8 %copy-done.3 = f32[8,8,128]{2,1,0:T(8,128)S(1)} copy-done((f32[8,8,128]{2,1,0:T(8,128)S(1)}, f32[8,8,128]{2,1,0:T(8,128)}, u32[]{:S(2)}) %copy-start.3) | copy-done | bytes 32792
  5.3 0.0 copy-start.5
  5.3 0.7 %copy-done.5 = f32[16,16]{1,0:T(8,128)S(1)} copy-done((f32[16,16]{1,0:T(8,128)S(1)}, f32[16,16]{1,0:T(8,128)}, u32[]{:S(2)}) %copy-start.5) | copy-done | bytes 1048
  6.0 0.0 copy-start.6
  6.0 0.7 %copy-done.6 = s32[8,128]{1,0:T(8,128)S(1)} copy-done((s32[8,128]{1,0:T(8,128)S(1)}, s32[8,128]{1,0:T(8,128)}, u32[]{:S(2)}) %copy-start.6) | copy-done | bytes 4120
  6.7 38.3 %shard_map.112 = (f32[16,128]{1,0:T(8,128)S(1)}, f32[1,16]{1,0:T(1,128)S(1)}, f32[256,512]{1,0:T(8,128)S(1)}) custom-call(s32[8,1]{1,0:T(8,128)S(1)} %copy.12.dest_ref, s32[16]{0:T(128)S(1)} %copy-done.7, f32[2,8,128]{2,1,0:T(8,128)S(1)} %copy-done.4, f32[8,8,128]{2,1,0:T(8,128)S(1)} %copy-done.3, s32[8,128]{1,0:T(8,128)S(1)} %copy-done.6, ...), custom_call_target="tpu_custom_call" | custom-call | flops 1000000000 | bytes 2200000 | tf_op jit(solution)/shard_map/pallas_call | solution.py:468
  45.0 0.6 %copy.16 = f32[16,128]{1,0:T(8,128)} copy(f32[16,128]{1,0:T(8,128)S(1)} %get-tuple-element.12) | data formatting | bytes 16384
  45.6 0.5 %copy.17 = f32[16]{0:T(128)} copy(f32[16]{0:T(128)S(1)} %bitcast.9) | data formatting | bytes 128
  46.1 0.8 %copy.18 = f32[2,8,16,512]{3,2,1,0:T(8,128)} copy(f32[2,8,16,512]{3,2,1,0:T(8,128)S(1)} %bitcast.5) | data formatting | bytes 1048576
Async XLA Ops:
  0.6 0.8 %copy-start.4 = (f32[2,8,128]{2,1,0:T(8,128)S(1)}, f32[2,8,128]{2,1,0:T(8,128)}, u32[]{:S(2)}) copy-start(f32[2,8,128]{2,1,0:T(8,128)} %residual_ref.1) | copy-start | bytes 24580
  0.6 0.8 %copy-start.7 = (s32[16]{0:T(128)S(1)}, s32[16]{0:T(128)}, u32[]{:S(2)}) copy-start(s32[16]{0:T(128)} %sources_ref.1) | copy-start | bytes 196
  1.4 1.0 %copy-start = (f32[2,8,16,512]{3,2,1,0:T(8,128)S(1)}, f32[2,8,16,512]{3,2,1,0:T(8,128)}, u32[]{:S(2)}) copy-start(f32[2,8,16,512]{3,2,1,0:T(8,128)} %param.13) | copy-start | bytes 1572868
  2.4 1.0 %copy-start.1 = (f32[2,8,16,512]{3,2,1,0:T(8,128)S(1)}, f32[2,8,16,512]{3,2,1,0:T(8,128)}, u32[]{:S(2)}) copy-start(f32[2,8,16,512]{3,2,1,0:T(8,128)} %param.14) | copy-start | bytes 1572868
  3.5 1.0 %copy-start.2 = (f32[2,8,16,512]{3,2,1,0:T(8,128)S(1)}, f32[2,8,16,512]{3,2,1,0:T(8,128)}, u32[]{:S(2)}) copy-start(f32[2,8,16,512]{3,2,1,0:T(8,128)} %param.15) | copy-start | bytes 1572868
  4.5 0.8 %copy-start.3 = (f32[8,8,128]{2,1,0:T(8,128)S(1)}, f32[8,8,128]{2,1,0:T(8,128)}, u32[]{:S(2)}) copy-start(f32[8,8,128]{2,1,0:T(8,128)} %kernel_ref.1) | copy-start | bytes 98308
  5.3 0.7 %copy-start.5 = (f32[16,16]{1,0:T(8,128)S(1)}, f32[16,16]{1,0:T(8,128)}, u32[]{:S(2)}) copy-start(f32[16,16]{1,0:T(8,128)} %gram_ref.1) | copy-start | bytes 3076
  6.0 0.7 %copy-start.6 = (s32[8,128]{1,0:T(8,128)S(1)}, s32[8,128]{1,0:T(8,128)}, u32[]{:S(2)}) copy-start(s32[8,128]{1,0:T(8,128)} %cells_ref.1) | copy-start | bytes 12292

commit v2 on v1

--- a/solution.py
+++ b/solution.py
@@ -22,16 +22,20 @@
     dims,
     dest_ref,
     sources_ref,
-    residual_ref,
-    kernel_ref,
-    cells_ref,
-    gram_ref,
+    residual_hbm,
+    kernel_hbm,
+    cells_hbm,
+    gram_hbm,
     wx_ref,
     wy_ref,
     mix_ref,
     grad_ref,
     coef_ref,
     adj_ref,
+    residual_ref,
+    kernel_ref,
+    cells_ref,
+    gram_ref,
     raw,
     coefs,
     states,
@@ -50,6 +54,7 @@
     send_pick,
     recv_pick,
     augmented,
+    small_sem,
     local_sem,
     obs_send,
     obs_recv,
@@ -72,6 +77,18 @@
     depth = members * levels
     log_columns = columns.bit_length() - 1
 
+    smalls = []
+    pairs = (
+        (residual_hbm, residual_ref),
+        (kernel_hbm, kernel_ref),
+        (cells_hbm, cells_ref),
+        (gram_hbm, gram_ref),
+    )
+    for which, (source, target) in enumerate(pairs):
+        copy = pltpu.make_async_copy(source, target, small_sem.at[which])
+        copy.start()
+        smalls.append(copy)
+
     loads = []
     for which, source in enumerate((wx_ref, wy_ref, mix_ref)):
         for j in range(strips):
@@ -97,6 +114,9 @@
 
     lax.fori_loop(1, tiles, greet_tile, 0)
     lax.fori_loop(1, groups, greet_ens, 0)
+
+    for copy in smalls:
+        copy.wait()
 
     def fill(tile, carry):
         def look(b, found):
@@ -472,9 +492,13 @@
             jax.ShapeDtypeStruct((1, nsrc), f32),
             jax.ShapeDtypeStruct(flat, f32),
         ),
-        in_specs=[smem, smem, vmem, vmem, vmem, vmem, anywhere, anywhere, anywhere],
+        in_specs=[smem, smem] + [anywhere] * 7,
         out_specs=(vmem, vmem, anywhere),
         scratch_shapes=[
+            pltpu.VMEM(residual.shape, f32),
+            pltpu.VMEM(kernel.shape, f32),
+            pltpu.VMEM(cell_ids.shape, jnp.int32),
+            pltpu.VMEM(gram_matrix.shape, f32),
             pltpu.VMEM((3, strips, flat[0], LANES), f32),
             pltpu.VMEM((edge_rows, 4, members, levels, columns), f32),
             pltpu.VMEM((STEPS + 1, state_rows, members, levels, columns), f32),
@@ -493,6 +517,7 @@
             pltpu.VMEM((nsrc, width), f32),
             pltpu.VMEM((tiles, nsrc, width), f32),
             pltpu.VMEM((nsrc, LANES), f32),
+            dma((4,)),
             dma((3, strips)),
             dma((tiles,)),
             dma((tiles,)),
@@ -507,7 +532,7 @@
             dma((strips,)),
         ],
         compiler_params=pltpu.CompilerParams(
-            collective_id=0, has_side_effects=True, vmem_limit_bytes=40 * 1024 * 1024
+            collective_id=0, has_side_effects=True, vmem_limit_bytes=63 * 1024 * 1024
         ),
         cost_estimate=pl.CostEstimate(
             flops=1_000_000_000, bytes_accessed=2_200_000, transcendentals=0

time: 47.3 us -> 44.8 us (0.947)
  local copies, waits for them, and re-layouts: 7.92 us -> 5.06 us
  Pallas kernels: 38.3 us -> 38.8 us
    unnamed x20 -> x10, local copies, waits for them, and re-layouts: 7.92 us -> 5.06 us
    pallas_call x1, Pallas kernels: 38.3 us -> 38.8 us  [per_device(): pl.pallas_call(functools.partial(body, dims), out_shape=(jax.ShapeDtypeSt...]
where the time goes in v2:
time: 44.8 us; the launch traced here: 44.5 us
  Pallas kernels  38.8 us (87%)
  local copies, waits for them, and re-layouts  5.06 us (11%)
  between operations  0.66 us (1%)
    pallas_call x1, Pallas kernels, per_device(): pl.pallas_call(functools.partial(body, dims), out_shape=(jax.ShapeDtypeSt...  38.8 us
    unnamed x10, local copies, waits for them, and re-layouts  5.06 us

profile of v2, /device:TPU:0, one launch (start us, length us, event | category | flops | bytes accessed | tf_op | source)
XLA Modules:
  0.0 44.5 jit_solution(514754686562460491)
XLA Ops:
  0.6 0.0 copy-start.1
  0.6 0.6 %copy-done.1 = s32[8,1]{0,1:T(1,128)S(1)} copy-done((s32[8,1]{0,1:T(1,128)S(1)}, s32[8,1]{0,1:T(1,128)}, u32[]{:S(2)}) %copy-start.1) | copy-done | bytes 56
  1.3 0.7 %copy.12.dest_ref = s32[8,1]{1,0:T(8,128)} copy(s32[8,1]{0,1:T(1,128)S(1)} %copy-done.1) | data formatting | bytes 64 | tf_op args[2]
  2.0 38.8 %shard_map.112 = (f32[16,128]{1,0:T(8,128)}, f32[1,16]{1,0:T(1,128)}, f32[256,512]{1,0:T(8,128)}) custom-call(s32[8,1]{1,0:T(8,128)} %copy.12.dest_ref, s32[16]{0:T(128)} %sources_ref.1, f32[2,8,128]{2,1,0:T(8,128)} %residual_hbm.1, f32[8,8,128]{2,1,0:T(8,128)} %kernel_hbm.1, s32[8,128]{1,0:T(8,128)} %cells_hbm.1, f32[16,16]{1,0:T(8,128)} %gram_hbm.1, ...), custom_call_target="tpu_custom_call" | custom-call | flops 1000000000 | bytes 2200000 | tf_op jit(solution)/shard_map/pallas_call | solution.py:488
  40.7 0.0 copy-start
  40.7 0.7 %copy-done = f32[16,128]{1,0:T(8,128)S(1)} copy-done((f32[16,128]{1,0:T(8,128)S(1)}, f32[16,128]{1,0:T(8,128)}, u32[]{:S(2)}) %copy-start) | copy-done | bytes 8216
  41.4 0.0 copy-start.2
  41.4 0.6 %copy.16 = f32[16,128]{1,0:T(8,128)} copy(f32[16,128]{1,0:T(8,128)S(1)} %copy-done) | data formatting | bytes 16384
  42.0 0.1 copy-done.2
  42.1 0.5 %copy.17 = f32[16]{0:T(128)} copy(f32[16]{0:T(128)S(1)} %bitcast.9) | data formatting | bytes 128
  42.6 1.9 %copy.18 = f32[2,8,16,512]{3,2,1,0:T(8,128)} copy(f32[2,8,16,512]{3,2,1,0:T(8,128)} %bitcast.5) | data formatting | bytes 1048576
Async XLA Ops:
  0.6 0.7 %copy-start.1 = (s32[8,1]{0,1:T(1,128)S(1)}, s32[8,1]{0,1:T(1,128)}, u32[]{:S(2)}) copy-start(s32[8,1]{0,1:T(1,128)} %param.11) | copy-start | bytes 100
  40.7 0.7 %copy-start = (f32[16,128]{1,0:T(8,128)S(1)}, f32[16,128]{1,0:T(8,128)}, u32[]{:S(2)}) copy-start(f32[16,128]{1,0:T(8,128)} %get-tuple-element.12) | copy-start | bytes 24580
  41.4 0.7 %copy-start.2 = (f32[1,16]{1,0:T(1,128)S(1)}, f32[1,16]{1,0:T(1,128)}, u32[]{:S(2)}) copy-start(f32[1,16]{1,0:T(1,128)} %get-tuple-element.7) | copy-start | bytes 196

commit v3 on v2

--- a/solution.py
+++ b/solution.py
@@ -189,6 +189,7 @@
     lane_iota = lax.broadcasted_iota(jnp.int32, (levels, LANES), 1)
 
     def prepare(x, carry):
+        made = []
         for m in range(members):
             at = pl.ds(m * levels * rows + x, levels, stride=rows)
             for j in range(strips):
@@ -201,11 +202,10 @@
                 if j == strips - 1:
                     wy = jnp.where((lane_iota == LANES - 1) & (wy > 0.0), 0.0, wy)
                 mixing = jnp.where(level_iota == levels - 1, 0.0, mixing)
-                lanes = slice(j * LANES, (j + 1) * LANES)
-                coefs[edge + x, 0, m, :, lanes] = center
-                coefs[edge + x, 1, m, :, lanes] = wx
-                coefs[edge + x, 2, m, :, lanes] = wy
-                coefs[edge + x, 3, m, :, lanes] = mixing
+                made.append((m, j, (center, wx, wy, mixing)))
+        for m, j, parts in made:
+            for which, value in enumerate(parts):
+                coefs[edge + x, which, m, :, j * LANES : (j + 1) * LANES] = value
         return carry
 
     lax.fori_loop(0, rows, prepare, 0)
@@ -279,13 +279,15 @@
     col_iota = lax.broadcasted_iota(jnp.int32, (nsrc, LANES), 1)
     augmented[...] = jnp.where(row_iota == col_iota, 1.0, 0.0)
     augmented[:, nsrc : 2 * nsrc] = gram_ref[...]
-    table = augmented[...]
-    for i in range(nsrc):
-        pivot = table[i : i + 1, :]
-        scaled = pivot / table[i : i + 1, nsrc + i : nsrc + i + 1]
-        column = table[:, nsrc + i : nsrc + i + 1]
-        table = jnp.where(row_iota == i, scaled, table - column * scaled)
-    augmented[...] = table
+
+    def eliminate(first, stop):
+        table = augmented[...]
+        for i in range(first, stop):
+            pivot = table[i : i + 1, :]
+            scaled = pivot / table[i : i + 1, nsrc + i : nsrc + i + 1]
+            column = table[:, nsrc + i : nsrc + i + 1]
+            table = jnp.where(row_iota == i, scaled, table - column * scaled)
+        augmented[...] = table
 
     def await_obs(d, carry):
         obs_copy(d).wait()
@@ -341,18 +343,10 @@
         lax.fori_loop(0, tiles // group, place, 0)
     states[0, HALO : HALO + rows] = forcing[...].reshape(rows, members, levels, columns)
 
-    for t in range(STEPS):
-        part = t % HALO
-        if part == 0:
-            start_both(functools.partial(halo_copy, t))
-            if t == 0 and edge:
-                await_both(edge_copy)
-            await_both(functools.partial(halo_copy, t))
-        reach = HALO - 1 - part
+    def advance_rows(t, chosen):
         last = t == STEPS - 1
-
-        def advance(r, carry):
-            summed = None
+        results = []
+        for r in chosen:
             for m in range(members):
                 here = states[t, r, m]
                 above = states[t, r + 1, m]
@@ -368,19 +362,45 @@
                 new += jnp.abs(wx) * jnp.where(wx > 0.0, above, below)
                 new += jnp.abs(wy) * jnp.where(wy > 0.0, right, left)
                 new += flux - roll(flux, 1, 0)
-                if last:
-                    at = pl.ds(m * levels * rows + r - HALO, levels, stride=rows)
-                    for j in range(strips):
-                        outbuf[j, at, :] = new[:, j * LANES : (j + 1) * LANES]
-                else:
-                    states[t + 1, r, m] = new
-                summed = new if summed is None else summed + new
-            if t > 0:
-                summed = summed + total[r]
+                results.append((r, m, new))
+        sums = []
+        for r in chosen:
+            summed = sum(new for row, _, new in results if row is r)
+            sums.append(summed + total[r] if t > 0 else summed)
+        for r, summed in zip(chosen, sums):
             total[r] = summed
+        for r, m, new in results:
+            if last:
+                at = pl.ds(m * levels * rows + r - HALO, levels, stride=rows)
+                for j in range(strips):
+                    outbuf[j, at, :] = new[:, j * LANES : (j + 1) * LANES]
+            else:
+                states[t + 1, r, m] = new
+
+    def advance_span(t, first, stop):
+        count = stop - first
+        unroll = next(u for u in (4, 3, 2, 1) if count % u == 0)
+
+        def one(i, carry):
+            start = first + i * unroll
+            advance_rows(t, [start + u for u in range(unroll)])
             return carry
 
-        lax.fori_loop(HALO - reach, HALO + rows + reach, advance, 0)
+        lax.fori_loop(0, count // unroll, one, 0)
+
+    for t in range(STEPS):
+        part = t % HALO
+        reach = HALO - 1 - part
+        if part == 0:
+            start_both(functools.partial(halo_copy, t))
+            advance_span(t, HALO + 1, HALO + rows - 1)
+            if t == 0 and edge:
+                await_both(edge_copy)
+            await_both(functools.partial(halo_copy, t))
+            advance_span(t, HALO - reach, HALO + 1)
+            advance_span(t, HALO + rows - 1, HALO + rows + reach)
+        else:
+            advance_span(t, HALO - reach, HALO + rows + reach)
 
     stores = []
     for j in range(strips):
@@ -420,6 +440,7 @@
     for d in range(1, groups):
         sum_copy(d).start()
     recv_sum[mine] = send_sum[mine]
+    eliminate(0, nsrc // 2)
     for d in range(1, groups):
         sum_copy(d).wait()
     summed = recv_sum[0]
@@ -448,6 +469,7 @@
 
     lax.fori_loop(1, tiles, start_pick, 0)
     recv_pick[me] = send_pick[...]
+    eliminate(nsrc // 2, nsrc)
 
     if edge:
         drain_both(edge_copy)

time: 44.8 us -> 37.7 us (0.84)
  Pallas kernels: 38.8 us -> 31.7 us
    pallas_call x1, Pallas kernels: 38.8 us -> 31.7 us  [per_device(): pl.pallas_call(functools.partial(body, dims), out_shape=(jax.ShapeDtypeSt...]
where the time goes in v3:
time: 37.7 us; the launch traced here: 37.4 us
  Pallas kernels  31.7 us (84%)
  local copies, waits for them, and re-layouts  5.06 us (13%)
  between operations  0.66 us (2%)
    pallas_call x1, Pallas kernels, per_device(): pl.pallas_call(functools.partial(body, dims), out_shape=(jax.ShapeDtypeSt...  31.7 us
    unnamed x10, local copies, waits for them, and re-layouts  5.06 us

profile of v3, /device:TPU:0, one launch (start us, length us, event | category | flops | bytes accessed | tf_op | source)
XLA Modules:
  0.0 37.4 jit_solution(15553879482998628958)
XLA Ops:
  0.6 0.0 copy-start.1
  0.6 0.6 %copy-done.1 = s32[8,1]{0,1:T(1,128)S(1)} copy-done((s32[8,1]{0,1:T(1,128)S(1)}, s32[8,1]{0,1:T(1,128)}, u32[]{:S(2)}) %copy-start.1) | copy-done | bytes 56
  1.3 0.7 %copy.12.dest_ref = s32[8,1]{1,0:T(8,128)} copy(s32[8,1]{0,1:T(1,128)S(1)} %copy-done.1) | data formatting | bytes 64 | tf_op args[2]
  2.0 31.7 %shard_map.112 = (f32[16,128]{1,0:T(8,128)}, f32[1,16]{1,0:T(1,128)}, f32[256,512]{1,0:T(8,128)}) custom-call(s32[8,1]{1,0:T(8,128)} %copy.12.dest_ref, s32[16]{0:T(128)} %sources_ref.1, f32[2,8,128]{2,1,0:T(8,128)} %residual_hbm.1, f32[8,8,128]{2,1,0:T(8,128)} %kernel_hbm.1, s32[8,128]{1,0:T(8,128)} %cells_hbm.1, f32[16,16]{1,0:T(8,128)} %gram_hbm.1, ...), custom_call_target="tpu_custom_call" | custom-call | flops 1000000000 | bytes 2200000 | tf_op jit(solution)/shard_map/pallas_call | solution.py:510
  33.6 0.0 copy-start
  33.6 0.7 %copy-done = f32[16,128]{1,0:T(8,128)S(1)} copy-done((f32[16,128]{1,0:T(8,128)S(1)}, f32[16,128]{1,0:T(8,128)}, u32[]{:S(2)}) %copy-start) | copy-done | bytes 8216
  34.3 0.0 copy-start.2
  34.3 0.6 %copy.16 = f32[16,128]{1,0:T(8,128)} copy(f32[16,128]{1,0:T(8,128)S(1)} %copy-done) | data formatting | bytes 16384
  34.9 0.1 copy-done.2
  35.0 0.5 %copy.17 = f32[16]{0:T(128)} copy(f32[16]{0:T(128)S(1)} %bitcast.9) | data formatting | bytes 128
  35.5 1.9 %copy.18 = f32[2,8,16,512]{3,2,1,0:T(8,128)} copy(f32[2,8,16,512]{3,2,1,0:T(8,128)} %bitcast.5) | data formatting | bytes 1048576
Async XLA Ops:
  0.6 0.7 %copy-start.1 = (s32[8,1]{0,1:T(1,128)S(1)}, s32[8,1]{0,1:T(1,128)}, u32[]{:S(2)}) copy-start(s32[8,1]{0,1:T(1,128)} %param.11) | copy-start | bytes 100
  33.6 0.7 %copy-start = (f32[16,128]{1,0:T(8,128)S(1)}, f32[16,128]{1,0:T(8,128)}, u32[]{:S(2)}) copy-start(f32[16,128]{1,0:T(8,128)} %get-tuple-element.12) | copy-start | bytes 24580
  34.3 0.7 %copy-start.2 = (f32[1,16]{1,0:T(1,128)S(1)}, f32[1,16]{1,0:T(1,128)}, u32[]{:S(2)}) copy-start(f32[1,16]{1,0:T(1,128)} %get-tuple-element.7) | copy-start | bytes 196
